TPU v7x, 32 devices: a whole 2x2x4 slice. The times are simulated.
32 devices in a mesh: seq: 8 (over z, x), fsdp: 4 (over y, core).
Axes of the slice: x: 2, y: 2, z: 4, core: 2. Of those that a mesh axis runs over, the one named last changes fastest.
Arguments:
- query_rows: bfloat16 [4096, 4096], P('seq', 'fsdp'), may hold values from -6 to 6
- key_rows: bfloat16 [4096, 4096], P('seq', 'fsdp'), may hold values from -0.5390625 to 0.5390625
- value_rows: bfloat16 [4096, 4096], P('seq', 'fsdp'), may hold values from -6 to 6
- norm_gain: float32 [4096], P('fsdp'), may hold values from 0.1 to 1.9
- out_weight: bfloat16 [4096, 4096], P(None, 'fsdp'), may hold values from -0.09375 to 0.09375
Outputs:
- mixed: bfloat16 [4096, 4096], P('seq', 'fsdp')
All inputs are finite; a program needn't handle non-finite values.
Results may differ from a plain program's by a relative error of at most 0.012.
Values may be sent and summed in bfloat16 or wider, within the bound.
A program may use at most 192 MiB of HBM per device.

v0:
```python
import jax
import jax.numpy as jnp
from jax import lax
from jax.sharding import PartitionSpec as P

DH = 128
BLK = 512


def entering(value, axis, combine, identity):
    count, index = (lax.axis_size(axis), lax.axis_index(axis))
    everything = lax.all_gather(value, axis)
    start = jnp.broadcast_to(jnp.asarray(identity, value.dtype), value.shape)

    def step(k, before):
        reached = k < index
        new = combine(before, everything[k])
        return jnp.where(reached, new, before)

    return lax.fori_loop(0, count, step, start)


def add_states(earlier, later):
    return earlier + later


def earlier_states(local_total):
    return entering(local_total, "seq", add_states, jnp.zeros_like(local_total))


def shards(query_rows, key_rows, value_rows, norm_gain, out_weight):
    tokens = query_rows.shape[0]
    feature_width = query_rows.shape[1]
    heads_here = feature_width // DH
    n_blocks = tokens // BLK
    highest = lax.Precision.HIGHEST
    queries_b = query_rows.reshape(n_blocks, BLK, heads_here, DH)
    keys_b = key_rows.reshape(n_blocks, BLK, heads_here, DH)
    values_b = value_rows.reshape(n_blocks, BLK, heads_here, DH)
    block_state = jnp.einsum(
        "nkhd,nkhe->nhde", keys_b, values_b, preferred_element_type=jnp.float32
    )
    local_total = jnp.sum(block_state, axis=0)
    running_sum = jnp.cumsum(block_state, axis=0)
    local_before = jnp.concatenate([jnp.zeros_like(block_state), running_sum[:-1]], axis=0)
    position = lax.broadcasted_iota(jnp.int32, (BLK, BLK), 0)
    column = lax.broadcasted_iota(jnp.int32, (BLK, BLK), 1)
    causal_mask = column <= position
    queries_f = queries_b.astype(jnp.float32)
    prefix = earlier_states(local_total)
    carried = prefix[None] + local_before
    from_state = jnp.einsum("nqhd,nhde->nqhe", queries_f, carried, precision=highest)
    scores = jnp.einsum("nqhd,nkhd->nhqk", queries_b, keys_b, preferred_element_type=jnp.float32)
    masked_scores = jnp.where(causal_mask[None, None], scores, 0.0).astype(jnp.bfloat16)
    attention = (
        jnp.einsum("nhqk,nkhd->nqhd", masked_scores, values_b, preferred_element_type=jnp.float32)
        + from_state
    )
    mean_square = jnp.mean(attention * attention, axis=-1, keepdims=True)
    normed = attention * lax.rsqrt(mean_square + 1e-06) * norm_gain.reshape(heads_here, DH)
    normed = normed.astype(jnp.bfloat16).reshape(tokens, feature_width)
    summed = jnp.dot(
        lax.all_gather(normed, "fsdp", axis=1, tiled=True),
        out_weight,
        preferred_element_type=jnp.float32,
    )
    return summed.astype(jnp.bfloat16)


def solution(mesh):
    placed = (P("seq", "fsdp"), P("seq", "fsdp"), P("seq", "fsdp"), P("fsdp"), P(None, "fsdp"))
    return jax.shard_map(
        shards, mesh=mesh, in_specs=placed, out_specs=P("seq", "fsdp"), check_vma=False
    )
```

profile of v0, /device:TPU:25, one launch (start us, length us, event | category | flops | bytes accessed | tf_op | source)
XLA Modules:
  0.0 156.6 jit_solution(5746295515952065084)
XLA Ops:
  6.5 0.0 copy-start
  6.5 0.0 all-gather.6.cloned.1.call-start
  6.5 1.6 %copy.17 = bf16[512,1024]{0,1:T(8,128)(2,1)S(1)} copy(bf16[512,1024]{1,0:T(8,128)(2,1)} %param.8) | data formatting | bytes 2097152 | tf_op jit(solution)/shard_map/reshape.2
  8.1 2.5 %fusion.9 = f32[8,128,128]{2,1,0:T(8,128)} fusion(bf16[512,8,128]{0,2,1:T(8,128)(2,1)S(1)} %bitcast.56, bf16[512,1024]{1,0:T(8,128)(2,1)} %param.9), kind=kOutput, calls=%fused_computation.14 | convolution fusion | flops 134217728 | bytes 2621440 | tf_op jit(solution)/shard_map/nkhd,nkhe->nhde/dot_general | solution.py:40
  10.6 0.0 all-gather.6.cloned.1.call-update
  10.6 0.0 all-gather.4.cloned.1.call-start
  10.7 0.1 iota_compare_fusion
  10.8 72.8 %all-gather.6.cloned.1.call-done = f32[64,128,128]{2,1,0:T(8,128)} async-done(((f32[8,128,128]{2,1,0:T(8,128)}), f32[64,128,128]{2,1,0:T(8,128)}) %all-gather.6.cloned.1.call-update) | async-done | bytes 4194320 | tf_op jit(solution)/shard_map/all_gather | solution.py:12
  83.6 10.0 %while.14 = (s32[]{:T(128)}, f32[8,128,128]{2,1,0:T(8,128)S(1)}, s32[]{:T(128)}, f32[8,8,128,128]{3,2,1,0:T(8,128)}, s32[]{:T(128)}, /*index=5*/s32[]{:T(128)}) while((s32[]{:T(128)}, f32[8,128,128]{2,1,0:T(8,128)S(1)}, s32[]{:T(128)}, f32[8,8,128,128]{3,2,1,0:T(8,128)}, s32[]{:T(128)}, /*index=5*/s32[]{:T(128)}) %tuple.40), condition=%wide.region_1.0_spmd.clone, body=%wide.region_0.0_spmd.clone.sunk | while | flops 393220 | bytes 1572957 | solution.py:20
  83.6 1.2 add_select_fusion.2
  84.8 1.2 add_select_fusion.2
  86.1 1.2 add_select_fusion.2
  87.3 1.2 add_select_fusion.2
  88.6 1.2 add_select_fusion.2
  89.8 1.2 add_select_fusion.2
  91.1 1.2 add_select_fusion.2
  92.3 1.2 add_select_fusion.2
  93.6 0.0 copy-done
  93.6 2.4 %fusion.13 = f32[8,128,512]{2,1,0:T(8,128)} fusion(f32[8,128,128]{2,1,0:T(8,128)S(1)} %get-tuple-element.84, bf16[512,1024]{1,0:T(8,128)(2,1)S(1)} %copy-done), kind=kOutput, calls=%fused_computation.17 | convolution fusion | flops 805306368 | bytes 3670016 | tf_op jit(solution)/shard_map/nqhd,nhde->nqhe/dot_general | solution.py:52
  96.0 0.0 copy-start.1
  96.0 5.9 %fusion.5 = (f32[512,8]{0,1:T(8,128)S(1)}, f32[8,128,512]{2,1,0:T(8,128)}) fusion(f32[8,128,512]{2,1,0:T(8,128)} %fusion.13, pred[512,512]{1,0:T(8,128)(4,1)S(1)} %iota_compare_fusion, bf16[512,8,128]{0,2,1:T(8,128)(2,1)S(1)} %bitcast.57, bf16[512,1024]{1,0:T(8,128)(2,1)} %param.9, bf16[512,1024]{1,0:T(8,128)(2,1)S(1)} %copy-done), kind=kOutput, calls=%fused_computation.8 | convolution fusion | flops 1079504896 | bytes 7618560 | tf_op jit(solution)/shard_map/nhqk,nkhd->nqhd/dot_general | solution.py:56
  101.8 0.0 copy-done.1
  101.9 2.8 %fusion.7 = bf16[1,512,8,128]{1,3,2,0:T(8,128)(2,1)} fusion(f32[8,128,512]{2,1,0:T(8,128)} %get-tuple-element.109, f32[8,128]{1,0:T(8,128)S(1)} %bitcast.60, f32[512,8]{0,1:T(8,128)S(1)} %add_rsqrt_fusion), kind=kLoop, calls=%fused_computation.10 | loop fusion | flops 1572864 | bytes 3166208 | tf_op jit(solution)/shard_map/convert_element_type | solution.py:61
  104.7 0.0 all-gather.4.cloned.1.call-update
  104.7 34.9 %all-gather.4.cloned.1.call-done = bf16[512,4096]{0,1:T(8,128)(2,1)} async-done(((bf16[512,1024]{0,1:T(8,128)(2,1)}), bf16[512,4096]{0,1:T(8,128)(2,1)}) %all-gather.4.cloned.1.call-update) | async-done | bytes 4194320 | tf_op jit(solution)/shard_map/all_gather | solution.py:63
  139.6 10.1 %convolution_convert_fusion = bf16[512,1024]{1,0:T(8,128)(2,1)} fusion(bf16[512,4096]{0,1:T(8,128)(2,1)} %all-gather.4.cloned.1.call-done, bf16[4096,1024]{1,0:T(8,128)(2,1)} %param.11), kind=kOutput, calls=%fused_computation.12 | convolution fusion | flops 4295491584 | bytes 13631488 | tf_op jit(solution)/shard_map/dot_general | solution.py:62
  (2 shorter events, 0.0 us)
Async XLA Ops:
  6.5 87.0 %copy-start = (bf16[512,1024]{1,0:T(8,128)(2,1)S(1)}, bf16[512,1024]{1,0:T(8,128)(2,1)}, u32[]{:S(2)}) copy-start(bf16[512,1024]{1,0:T(8,128)(2,1)} %param.7) | copy-start | bytes 3145732
  6.5 77.0 %all-gather.6.cloned.1.call-start = ((), (), s32[]{:S(2)}) async-start(), calls=%async_computation.1 | async-start | bytes 4718592 | tf_op jit(solution)/shard_map/all_gather | solution.py:12
  10.6 129.0 %all-gather.4.cloned.1.call-start = ((), (), s32[]{:S(2)}) async-start(), calls=%async_computation | async-start | bytes 5242880 | tf_op jit(solution)/shard_map/all_gather | solution.py:63
  96.0 5.9 %copy-start.1 = (f32[1024]{0:T(1024)S(1)}, f32[1024]{0:T(1024)}, u32[]{:S(2)}) copy-start(f32[1024]{0:T(1024)} %param.10) | copy-start | bytes 12292
Sparse Core Ops, SparseCore 0:
  10.8 72.7 all-gather.5
  104.8 34.7 all-gather.3
where the time goes:
time: 159 us; the launch traced here: 157 us
  waiting for transfers between devices  108 us (68%)
  matrix products  20.9 us (13%)
  between operations  13.5 us (8%)
  other arithmetic  12.7 us (8%)
  local copies, waits for them, and re-layouts  1.59 us (1%)
    all_gather x1, waiting for transfers between devices, entering(): everything = lax.all_gather(value, axis)  72.8 us
    all_gather x1, waiting for transfers between devices, shards(): lax.all_gather(normed, 'fsdp', axis=1, tiled=True)  34.9 us
    dot_general x1, matrix products, shards(): jnp.dot(lax.all_gather(normed, 'fsdp', axis=1, tiled=True), out_weight, p...  10.1 us
    select_n x8, other arithmetic, step(): return jnp.where(reached, new, before)  9.81 us
    dot_general x1, matrix products, shards(): jnp.einsum('nhqk,nkhd->nqhd', masked_scores, values_b, preferred_element_...  5.88 us
  transfers between devices with their start and end apart: 2, of which 2 were waited for; matrix products, arithmetic and copies ran while one was open for 0% of the time, Pallas kernels for 0%

commit v1 on v0

v1 whole, which is shorter than its diff:
```python
import functools

import jax
import jax.numpy as jnp
from jax import lax
from jax.experimental import pallas as pl
from jax.experimental.pallas import tpu as pltpu
from jax.sharding import PartitionSpec as P

DH = 128
TILE = 256
AHEAD = 2
MESH = pl.DeviceIdType.MESH
F32 = jnp.float32
BF16 = jnp.bfloat16


def dot(a, b, contract=((1,), (0,))):
    return lax.dot_general(a, b, (contract, ((), ())), preferred_element_type=F32)


def kernel(
    seq_n, q_hbm, k_hbm, v_hbm, gain_ref, w_hbm, o_ref,
    q, k, v, w, g, state, s_send, x_recv, c_send, c_recv, carry, within, acc,
    load_sem, w_sem, xs, xr, cs, cr, ss, sr, ys, yr, fs, fr,
):
    tokens, width = q.shape
    heads = width // DH
    i, f = lax.axis_index("seq"), lax.axis_index("fsdp")
    odd = lax.rem(i, 2)
    pair = i + 1 - 2 * odd
    sibling = f + 1 - 2 * lax.rem(f, 2)
    across = lax.rem(f + 2, 4)
    has_before = i >= 2
    has_after = i < seq_n - 2

    loads = [
        pltpu.make_async_copy(src, dst, load_sem.at[n])
        for n, (src, dst) in enumerate(((k_hbm, k), (v_hbm, v), (q_hbm, q)))
    ]
    for load in loads:
        load.start()
    w_loads = []
    for slot, source in enumerate((f, sibling, across, 3 - f)):
        rows = pl.ds(pl.multiple_of(source * width, width), width)
        w_loads.append(pltpu.make_async_copy(w_hbm.at[rows], w.at[slot], w_sem.at[slot]))

    barrier = pltpu.get_barrier_semaphore()

    def greet(j, e):
        pl.semaphore_signal(barrier, inc=1, device_id=(j, e), device_id_type=MESH)

    greet(pair, f)
    greet(i, sibling)
    greet(i, across)

    @pl.when(has_before)
    def _():
        greet(i - 2, f)

    @pl.when(has_after)
    def _():
        greet(i + 2, f)

    pl.semaphore_wait(barrier, 3 + has_before.astype(jnp.int32) + has_after.astype(jnp.int32))

    def remote(src, dst, send, recv, h, where):
        return pltpu.make_async_remote_copy(
            src_ref=src.at[h], dst_ref=dst.at[h], send_sem=send.at[h], recv_sem=recv.at[h],
            device_id=where, device_id_type=MESH,
        )

    after = lax.rem(i + 2, seq_n)
    to_pair = lambda h: remote(s_send, x_recv, xs, xr, h, (pair, f))
    to_after = lambda h: remote(c_send, c_recv, cs, cr, h, (after, f))
    to_sibling = lambda h: remote(g.at[0], g.at[1], ss, sr, h, (i, sibling))
    to_across = lambda h: remote(g.at[0], g.at[2], ys, yr, h, (i, across))
    pass_on = lambda h: remote(g.at[2], g.at[3], fs, fr, h, (i, sibling))

    loads[0].wait()
    loads[1].wait()
    for h in range(heads):
        columns = slice(h * DH, (h + 1) * DH)
        s = dot(k[:, columns], v[:, columns], ((0,), (0,)))
        state[h] = s
        s_send[h] = s.astype(BF16)
        to_pair(h).start()
    for load in w_loads:
        load.start()
    loads[2].wait()

    def head_step(h, _):
        columns = pl.ds(pl.multiple_of(h * DH, DH), DH)
        for r in range(tokens // TILE):
            rows = slice(r * TILE, (r + 1) * TILE)
            scores = dot(q[rows, columns], k[: (r + 1) * TILE, columns], ((1,), (1,)))
            row = lax.broadcasted_iota(jnp.int32, scores.shape, 0) + r * TILE
            column = lax.broadcasted_iota(jnp.int32, scores.shape, 1)
            masked = jnp.where(column <= row, scores, 0.0).astype(BF16)
            within[rows] = dot(masked, v[: (r + 1) * TILE, columns])

        to_pair(h).wait_recv()
        other = x_recv[h].astype(F32)
        total = state[h] + other
        mine = jnp.where(odd == 1, other, 0.0)

        @pl.when(has_before)
        def _():
            to_after(h).wait_recv()

            @pl.when(has_after)
            def _():
                c_send[h] = (total + c_recv[h].astype(F32)).astype(BF16)

            carry[...] = (mine + c_recv[h].astype(F32)).astype(BF16)

        @pl.when(jnp.logical_not(has_before))
        def _():
            c_send[h] = total.astype(BF16)
            carry[...] = mine.astype(BF16)

        @pl.when(has_after)
        def _():
            to_after(h).start()

        attention = within[...] + dot(q[:, columns], carry[...])
        mean_square = jnp.mean(attention * attention, axis=-1, keepdims=True)
        normed = attention * lax.rsqrt(mean_square + 1e-06) * gain_ref[:, columns]
        g[0, h] = normed.astype(BF16)
        to_sibling(h).start()

        @pl.when(h < AHEAD)
        def _():
            to_across(h).start()

        return 0

    lax.fori_loop(0, heads, head_step, 0)

    def whole_slot(slot, fresh):
        for n in range(0, acc.shape[1], TILE):
            columns = slice(n, n + TILE)
            part = None if fresh else acc[:, columns]
            for h in range(0, heads, 2):
                lhs = jnp.concatenate([g[slot, h], g[slot, h + 1]], axis=1)
                new = dot(lhs, w[slot, h * DH : (h + 2) * DH, columns])
                part = new if part is None else part + new
            acc[:, columns] = part

    w_loads[0].wait()
    whole_slot(0, True)
    w_loads[1].wait()

    def sibling_step(h, _):
        to_sibling(h).wait_recv()
        return 0

    lax.fori_loop(0, heads, sibling_step, 0)
    whole_slot(1, False)
    w_loads[2].wait()
    w_loads[3].wait()

    def arrive(h):
        to_across(h).wait_recv()
        pass_on(h).start()

        @pl.when(h + AHEAD < heads)
        def _():
            to_across(h).wait_send()
            to_across(h + AHEAD).start()

    def rows_of(slot, h):
        return w[slot, pl.ds(pl.multiple_of(h * DH, DH), DH)]

    arrive(jnp.int32(0))
    acc[...] += dot(g[2, 0], w[2, :DH])

    def across_step(h, _):
        arrive(h)
        pass_on(h - 1).wait_recv()
        lhs = jnp.concatenate([g[2, h], g[3, h - 1]], axis=1)
        rhs = jnp.concatenate([rows_of(2, h), rows_of(3, h - 1)], axis=0)
        acc[...] += dot(lhs, rhs)
        return 0

    lax.fori_loop(1, heads, across_step, 0)
    pass_on(heads - 1).wait_recv()
    last = dot(g[3, heads - 1], w[3, (heads - 1) * DH :])
    o_ref[...] = (acc[...] + last).astype(BF16)

    def drain(h, _):
        to_pair(h).wait_send()
        to_sibling(h).wait_send()
        pass_on(h).wait_send()

        @pl.when(h + AHEAD >= heads)
        def _():
            to_across(h).wait_send()

        @pl.when(has_after)
        def _():
            to_after(h).wait_send()

        return 0

    lax.fori_loop(0, heads, drain, 0)


def shards(seq_n, query_rows, key_rows, value_rows, norm_gain, out_weight):
    tokens, width = query_rows.shape
    heads = width // DH
    features = out_weight.shape[1]
    hbm = pl.BlockSpec(memory_space=pl.ANY)
    vmem = pl.BlockSpec(memory_space=pltpu.VMEM)
    small = (heads, DH, DH)
    return pl.pallas_call(
        functools.partial(kernel, seq_n),
        out_shape=jax.ShapeDtypeStruct((tokens, features), BF16),
        in_specs=[hbm, hbm, hbm, vmem, hbm],
        out_specs=vmem,
        scratch_shapes=[
            pltpu.VMEM((tokens, width), BF16),
            pltpu.VMEM((tokens, width), BF16),
            pltpu.VMEM((tokens, width), BF16),
            pltpu.VMEM((4, width, features), BF16),
            pltpu.VMEM((4, heads, tokens, DH), BF16),
            pltpu.VMEM(small, F32),
            pltpu.VMEM(small, BF16),
            pltpu.VMEM(small, BF16),
            pltpu.VMEM(small, BF16),
            pltpu.VMEM(small, BF16),
            pltpu.VMEM((DH, DH), BF16),
            pltpu.VMEM((tokens, DH), F32),
            pltpu.VMEM((tokens, features), F32),
            pltpu.SemaphoreType.DMA((3,)),
            pltpu.SemaphoreType.DMA((4,)),
        ]
        + [pltpu.SemaphoreType.DMA((heads,))] * 10,
        compiler_params=pltpu.CompilerParams(
            collective_id=0, has_side_effects=True, vmem_limit_bytes=48 * 1024 * 1024
        ),
        cost_estimate=pl.CostEstimate(
            flops=2 * tokens * width * 4 * features + 6 * tokens * tokens * width,
            bytes_accessed=2 * (4 * tokens * width + 4 * width * features),
            transcendentals=tokens * heads,
        ),
    )(query_rows, key_rows, value_rows, norm_gain.reshape(1, -1), out_weight)


def solution(mesh):
    placed = (P("seq", "fsdp"), P("seq", "fsdp"), P("seq", "fsdp"), P("fsdp"), P(None, "fsdp"))
    return jax.shard_map(
        functools.partial(shards, mesh.shape["seq"]),
        mesh=mesh, in_specs=placed, out_specs=P("seq", "fsdp"), check_vma=False,
    )
```

time: 159 us -> 50 us (0.31); the launches traced: 157 us -> 49.7 us
  waiting for transfers between devices: 108 us -> 0 us
  Pallas kernels: 0 us -> 44.4 us
  matrix products: 20.9 us -> 0 us
  between operations: 13.5 us -> 0.01 us
  other arithmetic: 12.7 us -> 0 us
  local copies, waits for them, and re-layouts: 1.59 us -> 5.33 us
    all_gather x2 -> x0, waiting for transfers between devices: 108 us -> none  [the longest x1 72.8 us: entering(): everything = lax.all_gather(value, axis)]
    pallas_call x0 -> x1, Pallas kernels: none -> 44.4 us  [shards(): pl.pallas_call(functools.partial(kernel, seq_n), out_shape=jax.ShapeDtype...]
    dot_general x4 -> x0, matrix products: 20.9 us -> none  [the longest x1 10.1 us: shards(): jnp.dot(lax.all_gather(normed, 'fsdp', axis=1, tiled=True), out_weight, p...]
    select_n x8 -> x0, other arithmetic: 9.81 us -> none  [step(): return jnp.where(reached, new, before)]
    unnamed x4 -> x9, local copies, waits for them, and re-layouts: 0.01 us -> 5.33 us
    convert_element_type x1 -> x0, other arithmetic: 2.84 us -> none  [shards(): normed = normed.astype(jnp.bfloat16).reshape(tokens, feature_width)]
  transfers between devices with their start and end apart: 2 -> 0, of which waited for: 2 -> 0; matrix products, arithmetic and copies ran while one was open for 0% -> 0% of each run, Pallas kernels for 0% -> 0%
where the time goes in v1:
time: 50 us; the launch traced here: 49.7 us
  Pallas kernels  44.4 us (89%)
  local copies, waits for them, and re-layouts  5.33 us (11%)
    pallas_call x1, Pallas kernels, shards(): pl.pallas_call(functools.partial(kernel, seq_n), out_shape=jax.ShapeDtype...  44.4 us
    unnamed x9, local copies, waits for them, and re-layouts  5.33 us

profile of v1, /device:TPU:25, one launch (start us, length us, event | category | flops | bytes accessed | tf_op | source)
XLA Modules:
  0.0 49.7 jit_solution(3799695131445396054)
XLA Ops:
  0.0 0.0 copy-start
  0.0 1.2 %copy-done = bf16[512,1024]{1,0:T(8,128)(2,1)S(1)} copy-done((bf16[512,1024]{1,0:T(8,128)(2,1)S(1)}, bf16[512,1024]{1,0:T(8,128)(2,1)}, u32[]{:S(2)}) %copy-start) | copy-done | bytes 1048600
  1.2 0.0 copy-start.1
  1.2 1.2 %copy-done.1 = bf16[512,1024]{1,0:T(8,128)(2,1)S(1)} copy-done((bf16[512,1024]{1,0:T(8,128)(2,1)S(1)}, bf16[512,1024]{1,0:T(8,128)(2,1)}, u32[]{:S(2)}) %copy-start.1) | copy-done | bytes 1048600
  2.5 0.0 copy-start.2
  2.5 1.2 %copy-done.2 = bf16[512,1024]{1,0:T(8,128)(2,1)S(1)} copy-done((bf16[512,1024]{1,0:T(8,128)(2,1)S(1)}, bf16[512,1024]{1,0:T(8,128)(2,1)}, u32[]{:S(2)}) %copy-start.2) | copy-done | bytes 1048600
  3.7 0.0 copy-start.3
  3.7 0.7 %copy-done.3 = f32[1024]{0:T(1024)S(1)} copy-done((f32[1024]{0:T(1024)S(1)}, f32[1024]{0:T(1024)}, u32[]{:S(2)}) %copy-start.3) | copy-done | bytes 4120
  4.4 44.4 %shard_map.55 = bf16[512,1024]{1,0:T(8,128)(2,1)S(1)} custom-call(bf16[512,1024]{1,0:T(8,128)(2,1)S(1)} %copy-done, bf16[512,1024]{1,0:T(8,128)(2,1)S(1)} %copy-done.1, bf16[512,1024]{1,0:T(8,128)(2,1)S(1)} %copy-done.2, f32[1,1024]{1,0:T(1,128)S(1)} %bitcast.1, bf16[4096,1024]{1,0:T(8,128)(2,1)} %w_hbm.1), custom_call_target="tpu_custom_call" | custom-call | flops 5905580032 | bytes 12582912 | tf_op jit(solution)/shard_map/pallas_call | solution.py:216
  48.8 1.0 %copy.7 = bf16[512,1024]{1,0:T(8,128)(2,1)} copy(bf16[512,1024]{1,0:T(8,128)(2,1)S(1)} %shard_map.55) | data formatting | bytes 2097152
Async XLA Ops:
  0.0 1.2 %copy-start = (bf16[512,1024]{1,0:T(8,128)(2,1)S(1)}, bf16[512,1024]{1,0:T(8,128)(2,1)}, u32[]{:S(2)}) copy-start(bf16[512,1024]{1,0:T(8,128)(2,1)} %q_hbm.1) | copy-start | bytes 3145732
  1.2 1.2 %copy-start.1 = (bf16[512,1024]{1,0:T(8,128)(2,1)S(1)}, bf16[512,1024]{1,0:T(8,128)(2,1)}, u32[]{:S(2)}) copy-start(bf16[512,1024]{1,0:T(8,128)(2,1)} %k_hbm.1) | copy-start | bytes 3145732
  2.5 1.2 %copy-start.2 = (bf16[512,1024]{1,0:T(8,128)(2,1)S(1)}, bf16[512,1024]{1,0:T(8,128)(2,1)}, u32[]{:S(2)}) copy-start(bf16[512,1024]{1,0:T(8,128)(2,1)} %v_hbm.1) | copy-start | bytes 3145732
  3.7 0.7 %copy-start.3 = (f32[1024]{0:T(1024)S(1)}, f32[1024]{0:T(1024)}, u32[]{:S(2)}) copy-start(f32[1024]{0:T(1024)} %param.8) | copy-start | bytes 12292

commit v2 on v1

--- a/solution.py
+++ b/solution.py
@@ -9,7 +9,7 @@
 
 DH = 128
 TILE = 256
-AHEAD = 2
+AHEAD = 4
 MESH = pl.DeviceIdType.MESH
 F32 = jnp.float32
 BF16 = jnp.bfloat16
@@ -237,7 +237,7 @@
         ]
         + [pltpu.SemaphoreType.DMA((heads,))] * 10,
         compiler_params=pltpu.CompilerParams(
-            collective_id=0, has_side_effects=True, vmem_limit_bytes=48 * 1024 * 1024
+            collective_id=0, has_side_effects=True, vmem_limit_bytes=62 * 1024 * 1024
         ),
         cost_estimate=pl.CostEstimate(
             flops=2 * tokens * width * 4 * features + 6 * tokens * tokens * width,

time: 50 us -> 42.6 us (0.85)
  Pallas kernels: 44.4 us -> 40.1 us
  local copies, waits for them, and re-layouts: 5.33 us -> 2.26 us
    pallas_call x1, Pallas kernels: 44.4 us -> 40.1 us  [shards(): pl.pallas_call(functools.partial(kernel, seq_n), out_shape=jax.ShapeDtype...]
    unnamed x9 -> x1, local copies, waits for them, and re-layouts: 5.33 us -> 2.26 us
where the time goes in v2:
time: 42.6 us; the launch traced here: 42.4 us
  Pallas kernels  40.1 us (94%)
  local copies, waits for them, and re-layouts  2.26 us (5%)
    pallas_call x1, Pallas kernels, shards(): pl.pallas_call(functools.partial(kernel, seq_n), out_shape=jax.ShapeDtype...  40.1 us
    unnamed x1, local copies, waits for them, and re-layouts  2.26 us

profile of v2, /device:TPU:25, one launch (start us, length us, event | category | flops | bytes accessed | tf_op | source)
XLA Modules:
  0.0 42.4 jit_solution(9535558321622648577)
XLA Ops:
  0.0 40.1 %shard_map.55 = bf16[512,1024]{1,0:T(8,128)(2,1)} custom-call(bf16[512,1024]{1,0:T(8,128)(2,1)} %q_hbm.1, bf16[512,1024]{1,0:T(8,128)(2,1)} %k_hbm.1, bf16[512,1024]{1,0:T(8,128)(2,1)} %v_hbm.1, f32[1,1024]{1,0:T(1,128)} %bitcast.1, bf16[4096,1024]{1,0:T(8,128)(2,1)} %w_hbm.1), custom_call_target="tpu_custom_call" | custom-call | flops 5905580032 | bytes 12582912 | tf_op jit(solution)/shard_map/pallas_call | solution.py:216
  40.1 2.3 %copy.7 = bf16[512,1024]{1,0:T(8,128)(2,1)} copy(bf16[512,1024]{1,0:T(8,128)(2,1)} %shard_map.55) | data formatting | bytes 2097152

commit v3 on v2

--- a/solution.py
+++ b/solution.py
@@ -10,6 +10,7 @@
 DH = 128
 TILE = 256
 AHEAD = 4
+EARLY = 3
 MESH = pl.DeviceIdType.MESH
 F32 = jnp.float32
 BF16 = jnp.bfloat16
@@ -20,9 +21,10 @@
 
 
 def kernel(
-    seq_n, q_hbm, k_hbm, v_hbm, gain_ref, w_hbm, o_ref,
+    seq_n, q_hbm, k_hbm, v_hbm, gain_hbm, w_hbm, o_ref,
     q, k, v, w, g, state, s_send, x_recv, c_send, c_recv, carry, within, acc,
-    load_sem, w_sem, xs, xr, cs, cr, ss, sr, ys, yr, fs, fr,
+    gain, far_gain, far_q, far_within, far_carry, within_send,
+    load_sem, w_sem, gain_sem, xs, xr, cs, cr, ss, sr, ys, yr, fs, fr, qs, qr, ws, wr,
 ):
     tokens, width = q.shape
     heads = width // DH
@@ -34,10 +36,15 @@
     has_before = i >= 2
     has_after = i < seq_n - 2
 
-    loads = [
-        pltpu.make_async_copy(src, dst, load_sem.at[n])
-        for n, (src, dst) in enumerate(((k_hbm, k), (v_hbm, v), (q_hbm, q)))
-    ]
+    early = jnp.minimum(i // 2, min(EARLY, heads // 2))
+    plain = heads - early
+    first, rest = pl.ds(0, 2 * DH), pl.ds(2 * DH, width - 2 * DH)
+    pieces = (
+        (k_hbm.at[:, first], k.at[:, first]), (v_hbm.at[:, first], v.at[:, first]),
+        (k_hbm.at[:, rest], k.at[:, rest]), (v_hbm.at[:, rest], v.at[:, rest]),
+        (q_hbm, q), (gain_hbm, gain),
+    )
+    loads = [pltpu.make_async_copy(src, dst, load_sem.at[n]) for n, (src, dst) in enumerate(pieces)]
     for load in loads:
         load.start()
     w_loads = []
@@ -77,20 +84,54 @@
     to_across = lambda h: remote(g.at[0], g.at[2], ys, yr, h, (i, across))
     pass_on = lambda h: remote(g.at[2], g.at[3], fs, fr, h, (i, sibling))
 
+    far = (i, across)
+
+    def across_copy(src, dst, send, recv):
+        return pltpu.make_async_remote_copy(
+            src_ref=src, dst_ref=dst, send_sem=send, recv_sem=recv, device_id=far, device_id_type=MESH
+        )
+
+    def columns_of(h):
+        return pl.ds(pl.multiple_of(h * DH, DH), DH)
+
+    gain_across = lambda: across_copy(gain_hbm, far_gain, gain_sem.at[0], gain_sem.at[1])
+
+    def q_across(h):
+        n = h - (heads - EARLY)
+        return across_copy(q_hbm.at[:, columns_of(h)], far_q.at[n], qs.at[n], qr.at[n])
+
+    def within_across(h):
+        n = h - (heads - EARLY)
+        return across_copy(within_send.at[n], far_within.at[n], ws.at[n], wr.at[n])
+
+    def carry_across(h):
+        return across_copy(carry.at[h], far_carry.at[h - (heads - EARLY)], ys.at[h], yr.at[h])
+
+    def start_early(h, _):
+        q_across(h).start()
+        return 0
+
     loads[0].wait()
     loads[1].wait()
     for h in range(heads):
+        if h == 2:
+            loads[2].wait()
+            loads[3].wait()
         columns = slice(h * DH, (h + 1) * DH)
         s = dot(k[:, columns], v[:, columns], ((0,), (0,)))
         state[h] = s
         s_send[h] = s.astype(BF16)
         to_pair(h).start()
+        if h == 0:
+            gain_across().start()
+            lax.fori_loop(plain, heads, start_early, 0)
     for load in w_loads:
         load.start()
-    loads[2].wait()
-
-    def head_step(h, _):
-        columns = pl.ds(pl.multiple_of(h * DH, DH), DH)
+    loads[4].wait()
+    loads[5].wait()
+
+    def form_within(h):
+        columns = columns_of(h)
         for r in range(tokens // TILE):
             rows = slice(r * TILE, (r + 1) * TILE)
             scores = dot(q[rows, columns], k[: (r + 1) * TILE, columns], ((1,), (1,)))
@@ -99,6 +140,21 @@
             masked = jnp.where(column <= row, scores, 0.0).astype(BF16)
             within[rows] = dot(masked, v[: (r + 1) * TILE, columns])
 
+    def early_step(h, _):
+        form_within(h)
+        within_send[h - (heads - EARLY)] = within[...].astype(BF16)
+        within_across(h).start()
+        return 0
+
+    lax.fori_loop(plain, heads, early_step, 0)
+
+    def normalize(attention, gains):
+        mean_square = jnp.mean(attention * attention, axis=-1, keepdims=True)
+        return (attention * lax.rsqrt(mean_square + 1e-06) * gains).astype(BF16)
+
+    def head_step(h, _):
+        columns = columns_of(h)
+        form_within(h)
         to_pair(h).wait_recv()
         other = x_recv[h].astype(F32)
         total = state[h] + other
@@ -112,24 +168,26 @@
             def _():
                 c_send[h] = (total + c_recv[h].astype(F32)).astype(BF16)
 
-            carry[...] = (mine + c_recv[h].astype(F32)).astype(BF16)
+            carry[h] = (mine + c_recv[h].astype(F32)).astype(BF16)
 
         @pl.when(jnp.logical_not(has_before))
         def _():
             c_send[h] = total.astype(BF16)
-            carry[...] = mine.astype(BF16)
+            carry[h] = mine.astype(BF16)
 
         @pl.when(has_after)
         def _():
             to_after(h).start()
 
-        attention = within[...] + dot(q[:, columns], carry[...])
-        mean_square = jnp.mean(attention * attention, axis=-1, keepdims=True)
-        normed = attention * lax.rsqrt(mean_square + 1e-06) * gain_ref[:, columns]
-        g[0, h] = normed.astype(BF16)
+        @pl.when(h >= plain)
+        def _():
+            carry_across(h).start()
+
+        attention = within[...] + dot(q[:, columns], carry[h])
+        g[0, h] = normalize(attention, gain[:, columns])
         to_sibling(h).start()
 
-        @pl.when(h < AHEAD)
+        @pl.when(jnp.logical_and(h < AHEAD, h < plain))
         def _():
             to_across(h).start()
 
@@ -160,42 +218,70 @@
     w_loads[2].wait()
     w_loads[3].wait()
 
+    gain_across().wait()
+
     def arrive(h):
-        to_across(h).wait_recv()
+        @pl.when(h >= plain)
+        def _():
+            q_across(h).wait_recv()
+            within_across(h).wait_recv()
+            carry_across(h).wait_recv()
+            n = h - (heads - EARLY)
+            attention = far_within[n].astype(F32) + dot(far_q[n], far_carry[n])
+            g[2, h] = normalize(attention, far_gain[:, columns_of(h)])
+
+        @pl.when(h < plain)
+        def _():
+            to_across(h).wait_recv()
+
         pass_on(h).start()
 
-        @pl.when(h + AHEAD < heads)
+        @pl.when(h + AHEAD < plain)
         def _():
             to_across(h).wait_send()
             to_across(h + AHEAD).start()
 
     def rows_of(slot, h):
-        return w[slot, pl.ds(pl.multiple_of(h * DH, DH), DH)]
-
-    arrive(jnp.int32(0))
-    acc[...] += dot(g[2, 0], w[2, :DH])
-
-    def across_step(h, _):
+        return w[slot, columns_of(h)]
+
+    def order(p):
+        return lax.rem(p + plain, heads)
+
+    start = order(0)
+    arrive(start)
+    acc[...] += dot(g[2, start], rows_of(2, start))
+
+    def across_step(p, _):
+        h, before = order(p), order(p - 1)
         arrive(h)
-        pass_on(h - 1).wait_recv()
-        lhs = jnp.concatenate([g[2, h], g[3, h - 1]], axis=1)
-        rhs = jnp.concatenate([rows_of(2, h), rows_of(3, h - 1)], axis=0)
+        pass_on(before).wait_recv()
+        lhs = jnp.concatenate([g[2, h], g[3, before]], axis=1)
+        rhs = jnp.concatenate([rows_of(2, h), rows_of(3, before)], axis=0)
         acc[...] += dot(lhs, rhs)
         return 0
 
     lax.fori_loop(1, heads, across_step, 0)
-    pass_on(heads - 1).wait_recv()
-    last = dot(g[3, heads - 1], w[3, (heads - 1) * DH :])
-    o_ref[...] = (acc[...] + last).astype(BF16)
+    final = order(heads - 1)
+    pass_on(final).wait_recv()
+    for n in range(0, acc.shape[1], TILE):
+        columns = slice(n, n + TILE)
+        last = dot(g[3, final], w[3, columns_of(final), columns])
+        o_ref[:, columns] = (acc[:, columns] + last).astype(BF16)
 
     def drain(h, _):
         to_pair(h).wait_send()
         to_sibling(h).wait_send()
         pass_on(h).wait_send()
 
-        @pl.when(h + AHEAD >= heads)
+        @pl.when(jnp.logical_and(h < plain, h + AHEAD >= plain))
         def _():
             to_across(h).wait_send()
+
+        @pl.when(h >= plain)
+        def _():
+            q_across(h).wait_send()
+            within_across(h).wait_send()
+            carry_across(h).wait_send()
 
         @pl.when(has_after)
         def _():
@@ -210,13 +296,13 @@
     tokens, width = query_rows.shape
     heads = width // DH
     features = out_weight.shape[1]
-    hbm = pl.BlockSpec(memory_space=pl.ANY)
+    hbm = pl.BlockSpec(memory_space=pltpu.HBM)
     vmem = pl.BlockSpec(memory_space=pltpu.VMEM)
     small = (heads, DH, DH)
     return pl.pallas_call(
         functools.partial(kernel, seq_n),
         out_shape=jax.ShapeDtypeStruct((tokens, features), BF16),
-        in_specs=[hbm, hbm, hbm, vmem, hbm],
+        in_specs=[hbm] * 5,
         out_specs=vmem,
         scratch_shapes=[
             pltpu.VMEM((tokens, width), BF16),
@@ -229,13 +315,21 @@
             pltpu.VMEM(small, BF16),
             pltpu.VMEM(small, BF16),
             pltpu.VMEM(small, BF16),
-            pltpu.VMEM((DH, DH), BF16),
+            pltpu.VMEM(small, BF16),
             pltpu.VMEM((tokens, DH), F32),
             pltpu.VMEM((tokens, features), F32),
-            pltpu.SemaphoreType.DMA((3,)),
+            pltpu.VMEM((1, width), F32),
+            pltpu.VMEM((1, width), F32),
+            pltpu.VMEM((EARLY, tokens, DH), BF16),
+            pltpu.VMEM((EARLY, tokens, DH), BF16),
+            pltpu.VMEM((EARLY, DH, DH), BF16),
+            pltpu.VMEM((EARLY, tokens, DH), BF16),
+            pltpu.SemaphoreType.DMA((6,)),
             pltpu.SemaphoreType.DMA((4,)),
+            pltpu.SemaphoreType.DMA((2,)),
         ]
-        + [pltpu.SemaphoreType.DMA((heads,))] * 10,
+        + [pltpu.SemaphoreType.DMA((heads,))] * 10
+        + [pltpu.SemaphoreType.DMA((EARLY,))] * 4,
         compiler_params=pltpu.CompilerParams(
             collective_id=0, has_side_effects=True, vmem_limit_bytes=62 * 1024 * 1024
         ),

time: 42.6 us -> 46.9 us (1.10)
  Pallas kernels: 40.1 us -> 44.5 us
    pallas_call x1, Pallas kernels: 40.1 us -> 44.5 us  [shards(): pl.pallas_call(functools.partial(kernel, seq_n), out_shape=jax.ShapeDtype...]
where the time goes in v3:
time: 46.9 us; the launch traced here: 46.8 us
  Pallas kernels  44.5 us (95%)
  local copies, waits for them, and re-layouts  2.26 us (5%)
    pallas_call x1, Pallas kernels, shards(): pl.pallas_call(functools.partial(kernel, seq_n), out_shape=jax.ShapeDtype...  44.5 us
    unnamed x1, local copies, waits for them, and re-layouts  2.26 us

profile of v3, /device:TPU:25, one launch (start us, length us, event | category | flops | bytes accessed | tf_op | source)
XLA Modules:
  0.0 46.8 jit_solution(2737807951381824123)
XLA Ops:
  0.0 44.5 %shard_map.55 = bf16[512,1024]{1,0:T(8,128)(2,1)} custom-call(bf16[512,1024]{1,0:T(8,128)(2,1)} %q_hbm.1, bf16[512,1024]{1,0:T(8,128)(2,1)} %k_hbm.1, bf16[512,1024]{1,0:T(8,128)(2,1)} %v_hbm.1, f32[1,1024]{1,0:T(1,128)} %bitcast.1, bf16[4096,1024]{1,0:T(8,128)(2,1)} %w_hbm.1), custom_call_target="tpu_custom_call" | custom-call | flops 5905580032 | bytes 12582912 | tf_op jit(solution)/shard_map/pallas_call | solution.py:302
  44.5 2.3 %copy.7 = bf16[512,1024]{1,0:T(8,128)(2,1)} copy(bf16[512,1024]{1,0:T(8,128)(2,1)} %shard_map.55) | data formatting | bytes 2097152

commit v4 on v3

--- a/solution.py
+++ b/solution.py
@@ -10,7 +10,7 @@
 DH = 128
 TILE = 256
 AHEAD = 4
-EARLY = 3
+EARLY = 2
 MESH = pl.DeviceIdType.MESH
 F32 = jnp.float32
 BF16 = jnp.bfloat16
@@ -37,7 +37,6 @@
     has_after = i < seq_n - 2
 
     early = jnp.minimum(i // 2, min(EARLY, heads // 2))
-    plain = heads - early
     first, rest = pl.ds(0, 2 * DH), pl.ds(2 * DH, width - 2 * DH)
     pieces = (
         (k_hbm.at[:, first], k.at[:, first]), (v_hbm.at[:, first], v.at[:, first]),
@@ -97,15 +96,13 @@
     gain_across = lambda: across_copy(gain_hbm, far_gain, gain_sem.at[0], gain_sem.at[1])
 
     def q_across(h):
-        n = h - (heads - EARLY)
-        return across_copy(q_hbm.at[:, columns_of(h)], far_q.at[n], qs.at[n], qr.at[n])
+        return across_copy(q_hbm.at[:, columns_of(h)], far_q.at[h], qs.at[h], qr.at[h])
 
     def within_across(h):
-        n = h - (heads - EARLY)
-        return across_copy(within_send.at[n], far_within.at[n], ws.at[n], wr.at[n])
+        return across_copy(within_send.at[h], far_within.at[h], ws.at[h], wr.at[h])
 
     def carry_across(h):
-        return across_copy(carry.at[h], far_carry.at[h - (heads - EARLY)], ys.at[h], yr.at[h])
+        return across_copy(carry.at[h], far_carry.at[h], ys.at[h], yr.at[h])
 
     def start_early(h, _):
         q_across(h).start()
@@ -122,9 +119,8 @@
         state[h] = s
         s_send[h] = s.astype(BF16)
         to_pair(h).start()
-        if h == 0:
-            gain_across().start()
-            lax.fori_loop(plain, heads, start_early, 0)
+    gain_across().start()
+    lax.fori_loop(0, early, start_early, 0)
     for load in w_loads:
         load.start()
     loads[4].wait()
@@ -142,11 +138,11 @@
 
     def early_step(h, _):
         form_within(h)
-        within_send[h - (heads - EARLY)] = within[...].astype(BF16)
+        within_send[h] = within[...].astype(BF16)
         within_across(h).start()
         return 0
 
-    lax.fori_loop(plain, heads, early_step, 0)
+    lax.fori_loop(0, early, early_step, 0)
 
     def normalize(attention, gains):
         mean_square = jnp.mean(attention * attention, axis=-1, keepdims=True)
@@ -179,7 +175,7 @@
         def _():
             to_after(h).start()
 
-        @pl.when(h >= plain)
+        @pl.when(h < early)
         def _():
             carry_across(h).start()
 
@@ -187,7 +183,7 @@
         g[0, h] = normalize(attention, gain[:, columns])
         to_sibling(h).start()
 
-        @pl.when(jnp.logical_and(h < AHEAD, h < plain))
+        @pl.when(jnp.logical_and(h >= early, h < early + AHEAD))
         def _():
             to_across(h).start()
 
@@ -221,22 +217,21 @@
     gain_across().wait()
 
     def arrive(h):
-        @pl.when(h >= plain)
+        @pl.when(h < early)
         def _():
             q_across(h).wait_recv()
             within_across(h).wait_recv()
             carry_across(h).wait_recv()
-            n = h - (heads - EARLY)
-            attention = far_within[n].astype(F32) + dot(far_q[n], far_carry[n])
+            attention = far_within[h].astype(F32) + dot(far_q[h], far_carry[h])
             g[2, h] = normalize(attention, far_gain[:, columns_of(h)])
 
-        @pl.when(h < plain)
+        @pl.when(h >= early)
         def _():
             to_across(h).wait_recv()
 
         pass_on(h).start()
 
-        @pl.when(h + AHEAD < plain)
+        @pl.when(jnp.logical_and(h >= early, h + AHEAD < heads))
         def _():
             to_across(h).wait_send()
             to_across(h + AHEAD).start()
@@ -244,15 +239,11 @@
     def rows_of(slot, h):
         return w[slot, columns_of(h)]
 
-    def order(p):
-        return lax.rem(p + plain, heads)
-
-    start = order(0)
-    arrive(start)
-    acc[...] += dot(g[2, start], rows_of(2, start))
-
-    def across_step(p, _):
-        h, before = order(p), order(p - 1)
+    arrive(jnp.int32(0))
+    acc[...] += dot(g[2, 0], w[2, :DH])
+
+    def across_step(h, _):
+        before = h - 1
         arrive(h)
         pass_on(before).wait_recv()
         lhs = jnp.concatenate([g[2, h], g[3, before]], axis=1)
@@ -261,11 +252,11 @@
         return 0
 
     lax.fori_loop(1, heads, across_step, 0)
-    final = order(heads - 1)
+    final = heads - 1
     pass_on(final).wait_recv()
     for n in range(0, acc.shape[1], TILE):
         columns = slice(n, n + TILE)
-        last = dot(g[3, final], w[3, columns_of(final), columns])
+        last = dot(g[3, final], w[3, final * DH :, columns])
         o_ref[:, columns] = (acc[:, columns] + last).astype(BF16)
 
     def drain(h, _):
@@ -273,11 +264,11 @@
         to_sibling(h).wait_send()
         pass_on(h).wait_send()
 
-        @pl.when(jnp.logical_and(h < plain, h + AHEAD >= plain))
+        @pl.when(jnp.logical_and(h >= early, h + AHEAD >= heads))
         def _():
             to_across(h).wait_send()
 
-        @pl.when(h >= plain)
+        @pl.when(h < early)
         def _():
             q_across(h).wait_send()
             within_across(h).wait_send()
@@ -331,7 +322,7 @@
         + [pltpu.SemaphoreType.DMA((heads,))] * 10
         + [pltpu.SemaphoreType.DMA((EARLY,))] * 4,
         compiler_params=pltpu.CompilerParams(
-            collective_id=0, has_side_effects=True, vmem_limit_bytes=62 * 1024 * 1024
+            collective_id=0, has_side_effects=True, vmem_limit_bytes=52 * 1024 * 1024
         ),
         cost_estimate=pl.CostEstimate(
             flops=2 * tokens * width * 4 * features + 6 * tokens * tokens * width,

time: 46.9 us -> 40.2 us (0.86)
  Pallas kernels: 44.5 us -> 38.3 us
  local copies, waits for them, and re-layouts: 2.26 us -> 1.66 us
    pallas_call x1, Pallas kernels: 44.5 us -> 38.3 us  [shards(): pl.pallas_call(functools.partial(kernel, seq_n), out_shape=jax.ShapeDtype...]
    unnamed x1 -> x3, local copies, waits for them, and re-layouts: 2.26 us -> 1.66 us
where the time goes in v4:
time: 40.2 us; the launch traced here: 39.9 us
  Pallas kernels  38.3 us (95%)
  local copies, waits for them, and re-layouts  1.66 us (4%)
    pallas_call x1, Pallas kernels, shards(): pl.pallas_call(functools.partial(kernel, seq_n), out_shape=jax.ShapeDtype...  38.3 us
    unnamed x3, local copies, waits for them, and re-layouts  1.66 us

profile of v4, /device:TPU:25, one launch (start us, length us, event | category | flops | bytes accessed | tf_op | source)
XLA Modules:
  0.0 39.9 jit_solution(12806324896212085486)
XLA Ops:
  0.0 0.0 copy-start
  0.0 0.7 %copy-done = f32[1024]{0:T(1024)S(1)} copy-done((f32[1024]{0:T(1024)S(1)}, f32[1024]{0:T(1024)}, u32[]{:S(2)}) %copy-start) | copy-done | bytes 4120
  0.7 38.3 %shard_map.55 = bf16[512,1024]{1,0:T(8,128)(2,1)S(1)} custom-call(bf16[512,1024]{1,0:T(8,128)(2,1)} %q_hbm.1, bf16[512,1024]{1,0:T(8,128)(2,1)} %k_hbm.1, bf16[512,1024]{1,0:T(8,128)(2,1)} %v_hbm.1, f32[1,1024]{1,0:T(1,128)S(1)} %bitcast.1, bf16[4096,1024]{1,0:T(8,128)(2,1)} %w_hbm.1), custom_call_target="tpu_custom_call" | custom-call | flops 5905580032 | bytes 12582912 | tf_op jit(solution)/shard_map/pallas_call | solution.py:293
  39.0 1.0 %copy.7 = bf16[512,1024]{1,0:T(8,128)(2,1)} copy(bf16[512,1024]{1,0:T(8,128)(2,1)S(1)} %shard_map.55) | data formatting | bytes 2097152
Async XLA Ops:
  0.0 0.7 %copy-start = (f32[1024]{0:T(1024)S(1)}, f32[1024]{0:T(1024)}, u32[]{:S(2)}) copy-start(f32[1024]{0:T(1024)} %param.8) | copy-start | bytes 12292

commit v5 on v4

--- a/solution.py
+++ b/solution.py
@@ -9,7 +9,8 @@
 
 DH = 128
 TILE = 256
-AHEAD = 4
+AHEAD = 3
+LEAD = 2
 EARLY = 2
 MESH = pl.DeviceIdType.MESH
 F32 = jnp.float32
@@ -36,7 +37,14 @@
     has_before = i >= 2
     has_after = i < seq_n - 2
 
-    early = jnp.minimum(i // 2, min(EARLY, heads // 2))
+    early = jnp.clip(i // 2 - 1, 0, EARLY)
+
+    def is_plain(h):
+        return jnp.logical_or(h < LEAD, h >= LEAD + early)
+
+    def follower(h):
+        return h + AHEAD + jnp.where(h < LEAD, early, 0)
+
     first, rest = pl.ds(0, 2 * DH), pl.ds(2 * DH, width - 2 * DH)
     pieces = (
         (k_hbm.at[:, first], k.at[:, first]), (v_hbm.at[:, first], v.at[:, first]),
@@ -96,13 +104,13 @@
     gain_across = lambda: across_copy(gain_hbm, far_gain, gain_sem.at[0], gain_sem.at[1])
 
     def q_across(h):
-        return across_copy(q_hbm.at[:, columns_of(h)], far_q.at[h], qs.at[h], qr.at[h])
+        return across_copy(q_hbm.at[:, columns_of(h)], far_q.at[h - LEAD], qs.at[h - LEAD], qr.at[h - LEAD])
 
     def within_across(h):
-        return across_copy(within_send.at[h], far_within.at[h], ws.at[h], wr.at[h])
+        return across_copy(within_send.at[h - LEAD], far_within.at[h - LEAD], ws.at[h - LEAD], wr.at[h - LEAD])
 
     def carry_across(h):
-        return across_copy(carry.at[h], far_carry.at[h], ys.at[h], yr.at[h])
+        return across_copy(carry.at[h], far_carry.at[h - LEAD], ys.at[h], yr.at[h])
 
     def start_early(h, _):
         q_across(h).start()
@@ -120,7 +128,7 @@
         s_send[h] = s.astype(BF16)
         to_pair(h).start()
     gain_across().start()
-    lax.fori_loop(0, early, start_early, 0)
+    lax.fori_loop(LEAD, LEAD + early, start_early, 0)
     for load in w_loads:
         load.start()
     loads[4].wait()
@@ -138,11 +146,11 @@
 
     def early_step(h, _):
         form_within(h)
-        within_send[h] = within[...].astype(BF16)
+        within_send[h - LEAD] = within[...].astype(BF16)
         within_across(h).start()
         return 0
 
-    lax.fori_loop(0, early, early_step, 0)
+    lax.fori_loop(LEAD, LEAD + early, early_step, 0)
 
     def normalize(attention, gains):
         mean_square = jnp.mean(attention * attention, axis=-1, keepdims=True)
@@ -175,7 +183,7 @@
         def _():
             to_after(h).start()
 
-        @pl.when(h < early)
+        @pl.when(jnp.logical_not(is_plain(h)))
         def _():
             carry_across(h).start()
 
@@ -183,7 +191,7 @@
         g[0, h] = normalize(attention, gain[:, columns])
         to_sibling(h).start()
 
-        @pl.when(jnp.logical_and(h >= early, h < early + AHEAD))
+        @pl.when(jnp.logical_and(is_plain(h), h < early + AHEAD))
         def _():
             to_across(h).start()
 
@@ -217,24 +225,24 @@
     gain_across().wait()
 
     def arrive(h):
-        @pl.when(h < early)
+        @pl.when(jnp.logical_not(is_plain(h)))
         def _():
             q_across(h).wait_recv()
             within_across(h).wait_recv()
             carry_across(h).wait_recv()
-            attention = far_within[h].astype(F32) + dot(far_q[h], far_carry[h])
+            attention = far_within[h - LEAD].astype(F32) + dot(far_q[h - LEAD], far_carry[h - LEAD])
             g[2, h] = normalize(attention, far_gain[:, columns_of(h)])
 
-        @pl.when(h >= early)
+        @pl.when(is_plain(h))
         def _():
             to_across(h).wait_recv()
 
         pass_on(h).start()
 
-        @pl.when(jnp.logical_and(h >= early, h + AHEAD < heads))
+        @pl.when(jnp.logical_and(is_plain(h), follower(h) < heads))
         def _():
             to_across(h).wait_send()
-            to_across(h + AHEAD).start()
+            to_across(follower(h)).start()
 
     def rows_of(slot, h):
         return w[slot, columns_of(h)]
@@ -264,11 +272,11 @@
         to_sibling(h).wait_send()
         pass_on(h).wait_send()
 
-        @pl.when(jnp.logical_and(h >= early, h + AHEAD >= heads))
+        @pl.when(jnp.logical_and(is_plain(h), follower(h) >= heads))
         def _():
             to_across(h).wait_send()
 
-        @pl.when(h < early)
+        @pl.when(jnp.logical_not(is_plain(h)))
         def _():
             q_across(h).wait_send()
             within_across(h).wait_send()

time: 40.2 us -> 40.1 us (level)
  no operation moved by 1% of the time
where the time goes in v5:
time: 40.1 us; the launch traced here: 40 us
  Pallas kernels  38.3 us (96%)
  local copies, waits for them, and re-layouts  1.66 us (4%)
    pallas_call x1, Pallas kernels, shards(): pl.pallas_call(functools.partial(kernel, seq_n), out_shape=jax.ShapeDtype...  38.3 us
    unnamed x3, local copies, waits for them, and re-layouts  1.66 us

profile of v5, /device:TPU:25, one launch (start us, length us, event | category | flops | bytes accessed | tf_op | source)
XLA Modules:
  0.0 40.0 jit_solution(17291138463391847838)
XLA Ops:
  0.0 0.0 copy-start
  0.0 0.7 %copy-done = f32[1024]{0:T(1024)S(1)} copy-done((f32[1024]{0:T(1024)S(1)}, f32[1024]{0:T(1024)}, u32[]{:S(2)}) %copy-start) | copy-done | bytes 4120
  0.7 38.3 %shard_map.55 = bf16[512,1024]{1,0:T(8,128)(2,1)S(1)} custom-call(bf16[512,1024]{1,0:T(8,128)(2,1)} %q_hbm.1, bf16[512,1024]{1,0:T(8,128)(2,1)} %k_hbm.1, bf16[512,1024]{1,0:T(8,128)(2,1)} %v_hbm.1, f32[1,1024]{1,0:T(1,128)S(1)} %bitcast.1, bf16[4096,1024]{1,0:T(8,128)(2,1)} %w_hbm.1), custom_call_target="tpu_custom_call" | custom-call | flops 5905580032 | bytes 12582912 | tf_op jit(solution)/shard_map/pallas_call | solution.py:301
  39.0 1.0 %copy.7 = bf16[512,1024]{1,0:T(8,128)(2,1)} copy(bf16[512,1024]{1,0:T(8,128)(2,1)S(1)} %shard_map.55) | data formatting | bytes 2097152
Async XLA Ops:
  0.0 0.7 %copy-start = (f32[1024]{0:T(1024)S(1)}, f32[1024]{0:T(1024)}, u32[]{:S(2)}) copy-start(f32[1024]{0:T(1024)} %param.8) | copy-start | bytes 12292

commit v6 on v5

--- a/solution.py
+++ b/solution.py
@@ -9,7 +9,7 @@
 
 DH = 128
 TILE = 256
-AHEAD = 3
+AHEAD = 4
 LEAD = 2
 EARLY = 2
 MESH = pl.DeviceIdType.MESH

time: 40.1 us -> 40.1 us (level)
  no operation moved by 1% of the time
where the time goes in v6:
time: 40.1 us; the launch traced here: 40 us
  Pallas kernels  38.3 us (96%)
  local copies, waits for them, and re-layouts  1.66 us (4%)
    pallas_call x1, Pallas kernels, shards(): pl.pallas_call(functools.partial(kernel, seq_n), out_shape=jax.ShapeDtype...  38.3 us
    unnamed x3, local copies, waits for them, and re-layouts  1.66 us

profile of v6, /device:TPU:25, one launch (start us, length us, event | category | flops | bytes accessed | tf_op | source)
XLA Modules:
  0.0 40.0 jit_solution(12785943594113546218)
XLA Ops:
  0.0 0.0 copy-start
  0.0 0.7 %copy-done = f32[1024]{0:T(1024)S(1)} copy-done((f32[1024]{0:T(1024)S(1)}, f32[1024]{0:T(1024)}, u32[]{:S(2)}) %copy-start) | copy-done | bytes 4120
  0.7 38.3 %shard_map.55 = bf16[512,1024]{1,0:T(8,128)(2,1)S(1)} custom-call(bf16[512,1024]{1,0:T(8,128)(2,1)} %q_hbm.1, bf16[512,1024]{1,0:T(8,128)(2,1)} %k_hbm.1, bf16[512,1024]{1,0:T(8,128)(2,1)} %v_hbm.1, f32[1,1024]{1,0:T(1,128)S(1)} %bitcast.1, bf16[4096,1024]{1,0:T(8,128)(2,1)} %w_hbm.1), custom_call_target="tpu_custom_call" | custom-call | flops 5905580032 | bytes 12582912 | tf_op jit(solution)/shard_map/pallas_call | solution.py:301
  39.0 1.0 %copy.7 = bf16[512,1024]{1,0:T(8,128)(2,1)} copy(bf16[512,1024]{1,0:T(8,128)(2,1)S(1)} %shard_map.55) | data formatting | bytes 2097152
Async XLA Ops:
  0.0 0.7 %copy-start = (f32[1024]{0:T(1024)S(1)}, f32[1024]{0:T(1024)}, u32[]{:S(2)}) copy-start(f32[1024]{0:T(1024)} %param.8) | copy-start | bytes 12292
